TPU v7x, 32 devices: a whole 2x2x4 slice. The times are simulated.
32 devices in a mesh: groups: 2 (over y), seq: 4 (over z), mp: 2 (over x), section: 2 (over core).
Axes of the slice: x: 2, y: 2, z: 4, core: 2. Of those that a mesh axis runs over, the one named last changes fastest.
Arguments:
- features: bfloat16 [16384, 128], P(('groups', 'seq', 'section')), parts along dimension 0, may hold values from -24 to 24
- flow_index: int32 [16384], P(('groups', 'seq', 'section')), parts along dimension 0, may hold values from 0 to 8191, as said below
- enc_weight: bfloat16 [128, 512], replicated, may hold values from -0.5 to 0.5
- q_weight: bfloat16 [512, 512], P(None, 'mp'), may hold values from -1 to 1
- k_weight: bfloat16 [512, 512], P(None, 'mp'), may hold values from -1 to 1
- v_weight: bfloat16 [512, 512], P(None, 'mp'), may hold values from -0.25 to 0.25
- upstream: int32 [8, 64, 4], P('mp', ('seq', 'section')), may hold values from -1 to 63, as said below
- grad_out: bfloat16 [16384, 512], P(('groups', 'seq', 'section'), 'mp'), parts along dimension 0, may hold values from -6 to 6
Outputs:
- attended: bfloat16 [16384, 512], P(('groups', 'seq', 'section'), 'mp'), parts along dimension 0
- q_grad: float32 [1024, 512], P('groups', 'mp'), parts along dimension 0
- k_grad: float32 [1024, 512], P('groups', 'mp'), parts along dimension 0
- v_grad: float32 [1024, 512], P('groups', 'mp'), parts along dimension 0
There are 2 independent parts, one for each index of `groups`. A program takes and returns all parts, laid end to end along the dimension named above; an argument that names none is the same for every part. Nothing has to cross between parts.
Inputs may be any that keep to these rules, and one draw needn't show every extreme that they name: `flow_index`: A permutation of the points. The rows j * 128 to (j + 1) * 128 - 1 of each point shard go to flow positions j * 1024 to (j + 1) * 1024 - 1. `upstream`: entry 0 of list (h, b) is b; every other entry is -1 (unused) or a block from b + 1 to b + 8, and the used entries of a list are distinct.
All inputs are finite; a program needn't handle non-finite values.
Results may differ from a plain program's by a relative error of at most 0.025.
The roundings to bfloat16 on the way count: a program that leaves them out, or rounds other values in their place, can miss the bound.
Values may be sent and summed in bfloat16 or wider, within the bound.
A program may use at most 64 MiB of HBM per device.

v0:
```python
import functools

import jax
import jax.numpy as jnp
from jax import lax
from jax.experimental import pallas as pl
from jax.experimental.pallas import tpu as pltpu
from jax.sharding import PartitionSpec as P

NT = (((1,), (1,)), ((), ()))
RING = ("seq", "section")
CHUNK = 512


def dot(a, b):
    return jnp.dot(a, b, preferred_element_type=jnp.float32)


def layer_kernel(
    up_ref, arrived_ref, places_ref, enc_ref, wq_ref, wk_ref, wv_ref, grad_ref,
    att_ref, gq_ref, gk_ref, gv_ref,
    normed_t, kv, kv_t, pairs, dq_t, *dkv,
):
    heads, blocks, slots = len(dkv), pairs.shape[0], 4
    points, width = grad_ref.shape
    hd = width // heads
    blk = points // blocks
    peers = lax.axis_size(RING)
    shard = lax.axis_index(RING)
    wkv = jnp.concatenate(
        [w[:, h * hd : (h + 1) * hd] for h in range(heads) for w in (wk_ref, wv_ref)], axis=1
    )
    no_weight = jnp.zeros((wq_ref.shape[0], hd), wq_ref.dtype)
    wq = jnp.concatenate(
        [w for h in range(heads) for w in (wq_ref[:, h * hd : (h + 1) * hd], no_weight)], axis=1
    )
    no_grad = jnp.zeros((points, hd), grad_ref.dtype)
    for h in range(heads):
        shifted = jnp.concatenate([no_grad, grad_ref[:, h * hd : (h + 1) * hd]], axis=1)
        pairs[:, h, blk:, :] = shifted.reshape(blocks, blk, 2 * hd)
        dkv[h][...] = jnp.zeros_like(dkv[h])

    for part in range(2):
        owner = lax.rem(shard + part, peers)
        place = places_ref[part] - owner * points
        for start in range(0, points, CHUNK):
            rows = lax.broadcasted_iota(jnp.int32, (CHUNK, points), 0) + start
            take = (rows == place).astype(jnp.float32).astype(jnp.bfloat16)
            flowed = dot(take, arrived_ref[part]).astype(jnp.bfloat16)
            encoded = jax.nn.gelu(dot(flowed, enc_ref[...])).astype(jnp.bfloat16)
            wide = encoded.astype(jnp.float32)
            mean = jnp.mean(wide * wide, axis=1, keepdims=True)
            normed = (wide * lax.rsqrt(mean + 1e-05)).astype(jnp.bfloat16)
            at = part * points + start
            normed_t[:, at : at + CHUNK] = normed.T
            projected = dot(normed, wkv).astype(jnp.bfloat16)
            turned = projected.T
            for i in range(CHUNK // blk):
                kv[at // blk + i] = projected[i * blk : (i + 1) * blk]
                kv_t[at // blk + i] = turned[:, i * blk : (i + 1) * blk]
            if part == 0:
                queries = dot(normed, wq).astype(jnp.bfloat16) * jnp.bfloat16(hd**-0.5)
                for i in range(CHUNK // blk):
                    for h in range(heads):
                        pairs[start // blk + i, h, :blk, :] = queries[
                            i * blk : (i + 1) * blk, h * 2 * hd : (h + 1) * 2 * hd
                        ]

    @pl.loop(0, blocks)
    def _(b):
        attended, query_grads = [], []
        for h in range(heads):
            index, bias = [], []
            for j in range(slots):
                entry = up_ref[(h * blocks + b) * slots + j]
                index.append(jnp.where(entry >= 0, entry - shard * blocks, 0))
                bias.append(jnp.where(entry >= 0, 0.0, -1e30).astype(jnp.float32))
            cols = slice(h * 2 * hd, (h + 1) * 2 * hd)
            keys = jnp.concatenate([kv[i, :, cols] for i in index], axis=0)
            keys_t = jnp.concatenate([kv_t[i, cols, :] for i in index], axis=1)
            pair = pairs[b, h]
            both = lax.dot_general(keys, pair, NT, preferred_element_type=jnp.float32)
            score = jnp.concatenate(
                [both[j * blk : (j + 1) * blk, :blk] + bias[j] for j in range(slots)], axis=0
            )
            prob_grad = both[:, blk:]
            e = jnp.exp(score - jnp.max(score, axis=0, keepdims=True))
            prob = e * (1.0 / jnp.sum(e, axis=0, keepdims=True))
            centre = jnp.sum(prob * prob_grad, axis=0, keepdims=True)
            score_grad = prob * (prob_grad - centre)
            narrow = jnp.concatenate(
                [score_grad.astype(jnp.bfloat16), prob.astype(jnp.bfloat16)], axis=1
            )
            back = dot(narrow, pair)
            for j in range(slots):
                dkv[h][index[j]] += back[j * blk : (j + 1) * blk]
            ahead = dot(keys_t, narrow)
            query_grads.append(ahead[:hd, :blk])
            attended.append(ahead[hd:, blk:])
        rows = pl.ds(pl.multiple_of(b * blk, blk), blk)
        att_ref[rows, :] = jnp.concatenate(attended, axis=0).T.astype(jnp.bfloat16)
        dq_t[b] = jnp.concatenate(query_grads, axis=0).astype(jnp.bfloat16)

    turned = jnp.concatenate([dq_t[b] for b in range(blocks)], axis=1)
    gq_ref[...] = lax.dot_general(
        normed_t[:, :points], turned, NT, preferred_element_type=jnp.float32
    ) * (hd**-0.5)
    for h in range(0, heads, 2):
        two = jnp.concatenate(
            [dkv[h + i][...].reshape(2 * points, 2 * hd).astype(jnp.bfloat16) for i in range(2)],
            axis=1,
        )
        g = dot(normed_t[...], two)
        cols = slice(h * hd, (h + 2) * hd)
        gk_ref[:, cols] = jnp.concatenate([g[:, :hd], g[:, 2 * hd : 3 * hd]], axis=1)
        gv_ref[:, cols] = jnp.concatenate([g[:, hd : 2 * hd], g[:, 3 * hd :]], axis=1)


def body(features, flow_index, enc_weight, q_weight, k_weight, v_weight, upstream, grad_out):
    points, fin = features.shape
    peers = lax.axis_size(RING)
    heads, blocks, slots = upstream.shape
    d, width = q_weight.shape
    hd = width // heads
    blk = points // blocks
    arrived = lax.all_to_all(
        features.reshape(peers, points // peers, fin), RING, split_axis=0, concat_axis=0, tiled=True
    ).reshape(points, fin)
    places = lax.all_to_all(
        flow_index.reshape(peers, points // peers), RING, split_axis=0, concat_axis=0, tiled=True
    ).reshape(1, points)
    back = [(i, i - 1) for i in range(1, peers)]
    arrived = jnp.stack([arrived, lax.ppermute(arrived, RING, back)])
    places = jnp.stack([places, lax.ppermute(places, RING, back)])
    vmem = pl.BlockSpec(memory_space=pltpu.VMEM)
    grads = jax.ShapeDtypeStruct((d, width), jnp.float32)
    attended, gq, gk, gv = pl.pallas_call(
        layer_kernel,
        out_shape=(jax.ShapeDtypeStruct((points, width), jnp.bfloat16), grads, grads, grads),
        in_specs=[pl.BlockSpec(memory_space=pltpu.SMEM)] + [vmem] * 7,
        out_specs=(vmem,) * 4,
        scratch_shapes=[
            pltpu.VMEM((d, 2 * points), jnp.bfloat16),
            pltpu.VMEM((2 * blocks, blk, 2 * width), jnp.bfloat16),
            pltpu.VMEM((2 * blocks, 2 * width, blk), jnp.bfloat16),
            pltpu.VMEM((blocks, heads, 2 * blk, 2 * hd), jnp.bfloat16),
            pltpu.VMEM((blocks, width, blk), jnp.bfloat16),
        ]
        + [pltpu.VMEM((2 * blocks, blk, 2 * hd), jnp.float32)] * heads,
        compiler_params=pltpu.CompilerParams(vmem_limit_bytes=50 << 20),
        name="layer",
    )(
        upstream.reshape(-1), arrived, places, enc_weight, q_weight, k_weight, v_weight, grad_out
    )
    return (attended,) + lax.psum((gq, gk, gv), RING)


def solution(mesh):
    return jax.shard_map(
        body,
        mesh=mesh,
        in_specs=(
            P(("groups", "seq", "section"), None),
            P(("groups", "seq", "section")),
            P(),
            P(None, "mp"),
            P(None, "mp"),
            P(None, "mp"),
            P("mp", ("seq", "section"), None),
            P(("groups", "seq", "section"), "mp"),
        ),
        out_specs=(
            P(("groups", "seq", "section"), "mp"),
            P("groups", "mp"),
            P("groups", "mp"),
            P("groups", "mp"),
        ),
        check_vma=False,
    )
```

profile of v0, /device:TPU:0, one launch (start us, length us, event | category | flops | bytes accessed | tf_op | source)
XLA Modules:
  0.0 141.3 jit_solution(13794040858749058164)
XLA Ops:
  7.2 0.0 all-reduce.3.cloned.1.call-start
  7.2 0.0 copy-start.8
  7.2 0.0 copy-start.3
  7.2 0.0 copy-start.4
  7.2 16.2 %all_to_all.14 = bf16[8,128,128]{2,1,0:T(8,128)(2,1)S(1)} all-to-all(bf16[8,128,128]{2,1,0:T(8,128)(2,1)} %bitcast.10), channel_id=1, replica_groups=mesh['groups'=2,'seq'=4,'mp'=2,'section'=2] {'seq','section'}, dimensions={0} | all-to-all | bytes 524288 | tf_op jit(solution)/shard_map/all_to_all | solution.py:126
  23.4 0.0 copy-start.7
  23.5 1.4 collective-permute-start
  24.9 0.0 copy-done.8
  24.9 8.6 %all_to_all.15 = s32[8,1,128]{2,1,0:T(1,128)S(1)} all-to-all(s32[8,1,128]{2,1,0:T(1,128)S(1)} %bitcast.14), channel_id=1, replica_groups=mesh['groups'=2,'seq'=4,'mp'=2,'section'=2] {'seq','section'}, dimensions={0} | all-to-all | bytes 8192 | tf_op jit(solution)/shard_map/all_to_all | solution.py:129
  33.5 1.3 collective-permute-start.1
  34.8 0.0 copy-done.7
  34.8 0.1 copy.14
  34.9 0.1 reshape.26.up_ref
  35.0 1.5 %collective-permute-done.1 = s32[1,1024]{1,0:T(1,128)S(1)} collective-permute-done((s32[1,1024]{1,0:T(1,128)S(1)}, s32[1,1024]{1,0:T(1,128)S(1)}, u32[]{:S(2)}, u32[]{:S(2)}) %collective-permute-start.1) | collective-permute-done | bytes 4128 | tf_op jit(solution)/shard_map/ppermute | solution.py:134
  36.6 0.0 collective-permute-done
  36.6 0.0 copy-start
  36.6 0.0 copy-start.1
  36.6 0.0 copy-start.2
  36.6 0.1 pad_maximum_fusion.arrived_ref
  36.7 0.0 copy-done.3
  36.7 0.0 copy-done.4
  36.7 0.9 copy-done
  37.6 0.1 copy-done.1
  37.7 0.1 copy-done.2
  37.8 30.8 %layer.1 = (bf16[1024,256]{1,0:T(8,128)(2,1)}, f32[512,256]{1,0:T(8,128)}, f32[512,256]{1,0:T(8,128)}, f32[512,256]{1,0:T(8,128)}) custom-call(s32[128]{0:T(128)S(1)} %reshape.26.up_ref, bf16[2,1024,128]{2,1,0:T(8,128)(2,1)S(1)} %pad_maximum_fusion.arrived_ref, s32[2,1,1024]{2,1,0:T(1,128)S(1)} %pad_add_fusion.places_ref, bf16[128,512]{1,0:T(8,128)(2,1)S(1)} %copy-done.4, ...), custom_call_target="tpu_custom_call" | custom-call | tf_op jit(solution)/shard_map/layer/pallas_call | solution.py:137
  68.6 0.0 all-reduce.3.cloned.1.call-update
  68.6 61.8 %all-reduce.3.cloned.1.call-done = (f32[512,256]{1,0:T(8,128)}, f32[512,256]{1,0:T(8,128)}, f32[512,256]{1,0:T(8,128)}) async-done(((f32[512,256]{1,0:T(8,128)}, f32[512,256]{1,0:T(8,128)}, f32[512,256]{1,0:T(8,128)}), (f32[512,256]{1,0:T(8,128)}, f32[512,256]{1,0:T(8,128)}, f32[512,256]{1,0:T(8,128)})) %all-reduce.3.cloned.1.call-update) | async-done | bytes 1572880 | tf_op jit(solution)/shard_map/psum | solution.py:155
  130.4 0.0 copy-start.6
  130.5 1.9 %copy.18 = f32[512,256]{1,0:T(8,128)} copy(f32[512,256]{1,0:T(8,128)} %get-tuple-element.16) | data formatting | bytes 1048576
  132.4 0.0 copy-done.6
  132.4 0.0 copy-start.5
  132.4 0.8 copy.19
  133.2 0.4 copy-done.5
  133.6 0.8 copy.20
  (1 shorter events, 0.0 us)
Async XLA Ops:
  7.2 123.3 %all-reduce.3.cloned.1.call-start = ((), (), s32[]{:S(2)}) async-start(), calls=%async_computation.2 | async-start | bytes 3145728 | tf_op jit(solution)/shard_map/psum | solution.py:155
  7.2 17.7 %copy-start.8 = (s32[1024]{0:T(1024)S(1)}, s32[1024]{0:T(1024)}, u32[]{:S(2)}) copy-start(s32[1024]{0:T(1024)} %param.9) | copy-start | bytes 12292
  7.2 29.4 %copy-start.3 = (bf16[512,256]{1,0:T(8,128)(2,1)S(1)}, bf16[512,256]{1,0:T(8,128)(2,1)}, u32[]{:S(2)}) copy-start(bf16[512,256]{1,0:T(8,128)(2,1)} %wv_ref.1) | copy-start | bytes 786436
  7.2 29.4 %copy-start.4 = (bf16[128,512]{1,0:T(8,128)(2,1)S(1)}, bf16[128,512]{1,0:T(8,128)(2,1)}, u32[]{:S(2)}) copy-start(bf16[128,512]{1,0:T(8,128)(2,1)} %enc_ref.1) | copy-start | bytes 393220
  23.4 11.4 %copy-start.7 = (s32[4,8,4]{1,2,0:T(4,128)S(1)}, s32[4,8,4]{1,2,0:T(4,128)}, u32[]{:S(2)}) copy-start(s32[4,8,4]{1,2,0:T(4,128)} %param.14) | copy-start | bytes 1540
  23.5 13.1 %collective-permute-start = (bf16[1024,128]{1,0:T(8,128)(2,1)S(1)}, bf16[1024,128]{1,0:T(8,128)(2,1)S(1)}, u32[]{:S(2)}, u32[]{:S(2)}) collective-permute-start(bf16[1024,128]{1,0:T(8,128)(2,1)S(1)} %bitcast.8), channel_id=1, source_target_pairs={{1,0},{4,1},{5,4},{8,5},{9,8},{12,9},{13,12},{3,2},{6,3},{7,6},{10... | collective-permute-start | bytes 786440 | tf_op jit(solution)/shard_map/ppermute | solution.py:133
  33.5 3.0 %collective-permute-start.1 = (s32[1,1024]{1,0:T(1,128)S(1)}, s32[1,1024]{1,0:T(1,128)S(1)}, u32[]{:S(2)}, u32[]{:S(2)}) collective-permute-start(s32[1,1024]{1,0:T(1,128)S(1)} %bitcast.12), channel_id=1, source_target_pairs={{1,0},{4,1},{5,4},{8,5},{9,8},{12,9},{13,12},{3,2},{6,3},{7,6},{10... | collective-permute-start | bytes 12296 | tf_op jit(solution)/shard_map/ppermute | solution.py:134
  36.6 1.0 copy-start
  36.6 1.1 copy-start.1
  36.6 1.2 copy-start.2
  130.4 1.9 %copy-start.6 = (f32[512,256]{1,0:T(8,128)S(1)}, f32[512,256]{1,0:T(8,128)}, u32[]{:S(2)}) copy-start(f32[512,256]{1,0:T(8,128)} %get-tuple-element.17) | copy-start | bytes 1572868
  132.4 1.2 copy-start.5
Sparse Core Ops, SparseCore 0:
  68.7 61.6 all-reduce.2
where the time goes:
time: 142 us; the launch traced here: 141 us
  waiting for transfers between devices  63.4 us (45%)
  Pallas kernels  30.8 us (22%)
  blocking collectives  24.8 us (17%)
  between operations  14.1 us (10%)
  local copies, waits for them, and re-layouts  5.26 us (4%)
  starting transfers between devices  2.73 us (2%)
    psum x1, waiting for transfers between devices, body(): return (attended,) + lax.psum((gq, gk, gv), RING)  61.8 us
    pallas_call x1, Pallas kernels, body(): pl.pallas_call(layer_kernel, out_shape=(jax.ShapeDtypeStruct((points, wid...  30.8 us
    all_to_all x1, blocking collectives, body(): lax.all_to_all(features.reshape(peers, points // peers, fin), RING, split...  16.2 us
    all_to_all x1, blocking collectives, body(): lax.all_to_all(flow_index.reshape(peers, points // peers), RING, split_ax...  8.63 us
    unnamed x22, local copies, waits for them, and re-layouts  5.16 us
  transfers between devices with their start and end apart: 3, of which 2 were waited for; matrix products, arithmetic and copies ran while one was open for 0% of the time, Pallas kernels for 0%

commit v1 on v0

--- a/solution.py
+++ b/solution.py
@@ -16,16 +16,210 @@
     return jnp.dot(a, b, preferred_element_type=jnp.float32)
 
 
+MESH = pl.DeviceIdType.MESH
+PIECES = 6
+
+
+def order_kernel(
+    rows_ref, index_ref, out_ref,
+    got, got_index, total, mine, following, sent, landed, sent_index, landed_index, halo,
+):
+    peers, pair, _ = got.shape
+    points = rows_ref.shape[0]
+    cores = lax.axis_size("section")
+    me = lax.axis_index(RING)
+
+    def device(i):
+        return {"seq": i // cores, "section": lax.rem(i, cores)}
+
+    def send(to, frm):
+        return (
+            pltpu.make_async_remote_copy(
+                rows_ref.at[pl.ds(pl.multiple_of(to * pair, pair), pair)], got.at[frm],
+                sent.at[to], landed.at[frm], device_id=device(to), device_id_type=MESH,
+            ),
+            pltpu.make_async_remote_copy(
+                index_ref.at[to], got_index.at[frm],
+                sent_index.at[to], landed_index.at[frm], device_id=device(to), device_id_type=MESH,
+            ),
+        )
+
+    def place(index, rows):
+        at = lax.broadcasted_iota(jnp.int32, (points, pair), 0)
+        return dot((at == index - me * points).astype(jnp.float32).astype(jnp.bfloat16), rows)
+
+    barrier = pltpu.get_barrier_semaphore()
+
+    @pl.loop(1, peers)
+    def _(i):
+        pl.semaphore_signal(
+            barrier, inc=1, device_id=device(lax.rem(me + i, peers)), device_id_type=MESH
+        )
+
+    pl.semaphore_wait(barrier, peers - 1)
+
+    @pl.loop(1, peers)
+    def _(i):
+        rows, index = send(lax.rem(me + i, peers), me)
+        index.start()
+        rows.start()
+
+    total[...] = place(index_ref[me], rows_ref[pl.ds(pl.multiple_of(me * pair, pair), pair), :])
+
+    @pl.loop(1, peers)
+    def _(i):
+        frm = lax.rem(me - i + peers, peers)
+        rows, index = send(frm, frm)
+        index.wait_recv()
+        rows.wait_recv()
+        total[...] += place(got_index[frm], got[frm])
+
+    mine[...] = total[...].astype(jnp.bfloat16)
+    before = lax.rem(me - 1 + peers, peers)
+    copy = pltpu.make_async_remote_copy(
+        mine, following, halo.at[0], halo.at[1], device_id=device(before), device_id_type=MESH
+    )
+    copy.start()
+    out_ref[0] = mine[...]
+
+    @pl.loop(1, peers)
+    def _(i):
+        rows, index = send(lax.rem(me + i, peers), me)
+        index.wait_send()
+        rows.wait_send()
+
+    copy.wait()
+    out_ref[1] = following[...]
+
+
+def sum_kernel(g_ref, out_ref, beside, part, up, cross, whole, *sems):
+    (
+        beside_sent, beside_got, inner_sent, up_got, cross_got,
+        outer_sent, outer_got, final_sent, final_got,
+    ) = sems
+    half = part.shape[0]
+    step = half // PIECES
+    chips = lax.axis_size("seq")
+    z, core = lax.axis_index("seq"), lax.axis_index("section")
+    base, other = core * half, (1 - core) * half
+    left = z < chips // 2
+    inner = jnp.where(left, z + 1, z - 1)
+    outer = jnp.where(left, z - 1, z + 1)
+    is_end = (z == 0) | (z == chips - 1)
+    is_mid = (z == chips // 2 - 1) | (z == chips // 2)
+    sibling = {"section": 1 - core}
+
+    def at(ref, first, t):
+        return ref.at[pl.ds(pl.multiple_of(first + t * step, step), step)]
+
+    def remote(src, dst, send_sem, recv_sem, t, to):
+        return pltpu.make_async_remote_copy(
+            src, dst, send_sem.at[t], recv_sem.at[t], device_id=to, device_id_type=MESH
+        )
+
+    def to_sibling(t):
+        return remote(at(g_ref, other, t), at(beside, 0, t), beside_sent, beside_got, t, sibling)
+
+    def to_inner(t, dst, got):
+        return remote(at(part, 0, t), at(dst, 0, t), inner_sent, got, t, {"seq": inner})
+
+    def to_outer(t):
+        return remote(at(whole, base, t), at(whole, base, t), outer_sent, outer_got, t, {"seq": outer})
+
+    def final(t, first):
+        return remote(at(whole, first, t), at(whole, first, t), final_sent, final_got, t, sibling)
+
+    barrier = pltpu.get_barrier_semaphore()
+    pl.semaphore_signal(barrier, inc=1, device_id=sibling, device_id_type=MESH)
+    pl.semaphore_signal(barrier, inc=1, device_id={"seq": inner}, device_id_type=MESH)
+
+    @pl.when(is_end)
+    def _():
+        pl.semaphore_wait(barrier, 2)
+
+    @pl.when(jnp.logical_not(is_end))
+    def _():
+        pl.semaphore_signal(barrier, inc=1, device_id={"seq": outer}, device_id_type=MESH)
+        pl.semaphore_wait(barrier, 3)
+
+    for t in range(PIECES):
+        to_sibling(t).start()
+
+    def inward(t):
+        to_sibling(t).wait_recv()
+        here = at(part, 0, t)
+        both = at(g_ref, base, t)[...].astype(jnp.float32) + at(beside, 0, t)[...].astype(jnp.float32)
+
+        @pl.when(is_end)
+        def _():
+            here[...] = both.astype(jnp.bfloat16)
+
+        @pl.when(jnp.logical_not(is_end))
+        def _():
+            to_inner(t, up, up_got).wait_recv()
+            here[...] = (both + at(up, 0, t)[...].astype(jnp.float32)).astype(jnp.bfloat16)
+
+        @pl.when(is_mid)
+        def _():
+            to_inner(t, cross, cross_got).start()
+
+        @pl.when(jnp.logical_not(is_mid))
+        def _():
+            to_inner(t, up, up_got).start()
+
+    def outward(t):
+        @pl.when(jnp.logical_not(is_end))
+        def _():
+            to_outer(t).start()
+
+        final(t, base).start()
+
+    for t in range(PIECES + 1):
+        if t < PIECES:
+            inward(t)
+        if t >= 1:
+
+            @pl.when(is_mid)
+            def _():
+                to_inner(t - 1, cross, cross_got).wait_recv()
+                at(whole, base, t - 1)[...] = (
+                    at(part, 0, t - 1)[...].astype(jnp.float32)
+                    + at(cross, 0, t - 1)[...].astype(jnp.float32)
+                ).astype(jnp.bfloat16)
+                outward(t - 1)
+
+    for t in range(PIECES):
+
+        @pl.when(jnp.logical_not(is_mid))
+        def _():
+            to_outer(t).wait_recv()
+            outward(t)
+
+    mine = pl.ds(pl.multiple_of(base, half), half)
+    out_ref[mine, :] = whole[mine, :]
+    for t in range(PIECES):
+        final(t, other).wait_recv()
+        rows = pl.ds(pl.multiple_of(other + t * step, step), step)
+        out_ref[rows, :] = whole[rows, :]
+    for t in range(PIECES):
+        to_sibling(t).wait_send()
+        to_inner(t, up, up_got).wait_send()
+        final(t, base).wait_send()
+
+        @pl.when(jnp.logical_not(is_end))
+        def _():
+            to_outer(t).wait_send()
+
+
 def layer_kernel(
-    up_ref, arrived_ref, places_ref, enc_ref, wq_ref, wk_ref, wv_ref, grad_ref,
-    att_ref, gq_ref, gk_ref, gv_ref,
+    up_ref, flowed_ref, enc_ref, wq_ref, wk_ref, wv_ref, grad_ref,
+    att_ref, g_ref,
     normed_t, kv, kv_t, pairs, dq_t, *dkv,
 ):
     heads, blocks, slots = len(dkv), pairs.shape[0], 4
     points, width = grad_ref.shape
     hd = width // heads
     blk = points // blocks
-    peers = lax.axis_size(RING)
     shard = lax.axis_index(RING)
     wkv = jnp.concatenate(
         [w[:, h * hd : (h + 1) * hd] for h in range(heads) for w in (wk_ref, wv_ref)], axis=1
@@ -41,12 +235,8 @@
         dkv[h][...] = jnp.zeros_like(dkv[h])
 
     for part in range(2):
-        owner = lax.rem(shard + part, peers)
-        place = places_ref[part] - owner * points
         for start in range(0, points, CHUNK):
-            rows = lax.broadcasted_iota(jnp.int32, (CHUNK, points), 0) + start
-            take = (rows == place).astype(jnp.float32).astype(jnp.bfloat16)
-            flowed = dot(take, arrived_ref[part]).astype(jnp.bfloat16)
+            flowed = flowed_ref[part, start : start + CHUNK, :]
             encoded = jax.nn.gelu(dot(flowed, enc_ref[...])).astype(jnp.bfloat16)
             wide = encoded.astype(jnp.float32)
             mean = jnp.mean(wide * wide, axis=1, keepdims=True)
@@ -102,18 +292,20 @@
         dq_t[b] = jnp.concatenate(query_grads, axis=0).astype(jnp.bfloat16)
 
     turned = jnp.concatenate([dq_t[b] for b in range(blocks)], axis=1)
-    gq_ref[...] = lax.dot_general(
-        normed_t[:, :points], turned, NT, preferred_element_type=jnp.float32
-    ) * (hd**-0.5)
+    d = enc_ref.shape[1]
+    g_ref[:d] = (
+        lax.dot_general(normed_t[:, :points], turned, NT, preferred_element_type=jnp.float32)
+        * (hd**-0.5)
+    ).astype(jnp.bfloat16)
     for h in range(0, heads, 2):
         two = jnp.concatenate(
             [dkv[h + i][...].reshape(2 * points, 2 * hd).astype(jnp.bfloat16) for i in range(2)],
             axis=1,
         )
-        g = dot(normed_t[...], two)
+        g = dot(normed_t[...], two).astype(jnp.bfloat16)
         cols = slice(h * hd, (h + 2) * hd)
-        gk_ref[:, cols] = jnp.concatenate([g[:, :hd], g[:, 2 * hd : 3 * hd]], axis=1)
-        gv_ref[:, cols] = jnp.concatenate([g[:, hd : 2 * hd], g[:, 3 * hd :]], axis=1)
+        g_ref[d : 2 * d, cols] = jnp.concatenate([g[:, :hd], g[:, 2 * hd : 3 * hd]], axis=1)
+        g_ref[2 * d :, cols] = jnp.concatenate([g[:, hd : 2 * hd], g[:, 3 * hd :]], axis=1)
 
 
 def body(features, flow_index, enc_weight, q_weight, k_weight, v_weight, upstream, grad_out):
@@ -123,22 +315,32 @@
     d, width = q_weight.shape
     hd = width // heads
     blk = points // blocks
-    arrived = lax.all_to_all(
-        features.reshape(peers, points // peers, fin), RING, split_axis=0, concat_axis=0, tiled=True
-    ).reshape(points, fin)
-    places = lax.all_to_all(
-        flow_index.reshape(peers, points // peers), RING, split_axis=0, concat_axis=0, tiled=True
-    ).reshape(1, points)
-    back = [(i, i - 1) for i in range(1, peers)]
-    arrived = jnp.stack([arrived, lax.ppermute(arrived, RING, back)])
-    places = jnp.stack([places, lax.ppermute(places, RING, back)])
+    pair = points // peers
+    dma = pltpu.SemaphoreType.DMA
     vmem = pl.BlockSpec(memory_space=pltpu.VMEM)
-    grads = jax.ShapeDtypeStruct((d, width), jnp.float32)
-    attended, gq, gk, gv = pl.pallas_call(
+    flowed = pl.pallas_call(
+        order_kernel,
+        out_shape=jax.ShapeDtypeStruct((2, points, fin), features.dtype),
+        in_specs=[vmem] * 2,
+        out_specs=vmem,
+        scratch_shapes=[
+            pltpu.VMEM((peers, pair, fin), features.dtype),
+            pltpu.VMEM((peers, 1, pair), jnp.int32),
+            pltpu.VMEM((points, fin), jnp.float32),
+            pltpu.VMEM((points, fin), features.dtype),
+            pltpu.VMEM((points, fin), features.dtype),
+            dma((peers,)), dma((peers,)), dma((peers,)), dma((peers,)), dma((2,)),
+        ],
+        compiler_params=pltpu.CompilerParams(
+            collective_id=0, has_side_effects=True, vmem_limit_bytes=30 << 20
+        ),
+        name="order",
+    )(features, flow_index.reshape(peers, 1, pair))
+    attended, partial = pl.pallas_call(
         layer_kernel,
-        out_shape=(jax.ShapeDtypeStruct((points, width), jnp.bfloat16), grads, grads, grads),
-        in_specs=[pl.BlockSpec(memory_space=pltpu.SMEM)] + [vmem] * 7,
-        out_specs=(vmem,) * 4,
+        out_shape=(jax.ShapeDtypeStruct((points, width), jnp.bfloat16), jax.ShapeDtypeStruct((3 * d, width), jnp.bfloat16)),
+        in_specs=[pl.BlockSpec(memory_space=pltpu.SMEM)] + [vmem] * 6,
+        out_specs=(vmem,) * 2,
         scratch_shapes=[
             pltpu.VMEM((d, 2 * points), jnp.bfloat16),
             pltpu.VMEM((2 * blocks, blk, 2 * width), jnp.bfloat16),
@@ -150,9 +352,23 @@
         compiler_params=pltpu.CompilerParams(vmem_limit_bytes=50 << 20),
         name="layer",
     )(
-        upstream.reshape(-1), arrived, places, enc_weight, q_weight, k_weight, v_weight, grad_out
-    )
-    return (attended,) + lax.psum((gq, gk, gv), RING)
+        upstream.reshape(-1), flowed, enc_weight, q_weight, k_weight, v_weight, grad_out
+    )
+    half = 3 * d // 2
+    summed = pl.pallas_call(
+        sum_kernel,
+        out_shape=jax.ShapeDtypeStruct((3 * d, width), jnp.bfloat16),
+        in_specs=[vmem],
+        out_specs=vmem,
+        scratch_shapes=[pltpu.VMEM((half, width), jnp.bfloat16)] * 4
+        + [pltpu.VMEM((3 * d, width), jnp.bfloat16)]
+        + [dma((PIECES,))] * 9,
+        compiler_params=pltpu.CompilerParams(
+            collective_id=1, has_side_effects=True, vmem_limit_bytes=30 << 20
+        ),
+        name="sum",
+    )(partial).astype(jnp.float32)
+    return (attended, summed[:d], summed[d : 2 * d], summed[2 * d :])
 
 
 def solution(mesh):

time: 142 us -> 75.8 us (0.53)
  waiting for transfers between devices: 63.4 us -> 0 us
  Pallas kernels: 30.8 us -> 68.3 us
  blocking collectives: 24.8 us -> 0 us
  between operations: 14.1 us -> 0.7 us
  starting transfers between devices: 2.73 us -> 0 us
    psum x1 -> x0, waiting for transfers between devices: 61.8 us -> none  [body(): return (attended,) + lax.psum((gq, gk, gv), RING)]
    pallas_call x0 -> x2, Pallas kernels: none -> 40.7 us  [the longest x1 25.4 us: body(): pl.pallas_call(sum_kernel, out_shape=jax.ShapeDtypeStruct((3 * d, width),...]
    all_to_all x2 -> x0, blocking collectives: 24.8 us -> none  [the longest x1 16.2 us: body(): lax.all_to_all(features.reshape(peers, points // peers, fin), RING, split...]
    pallas_call x1, Pallas kernels: 30.8 us -> 27.6 us  [body(): pl.pallas_call(layer_kernel, out_shape=(jax.ShapeDtypeStruct((points, wid...]
    ppermute x2 -> x0, starting transfers between devices: 2.69 us -> none  [the longest x1 1.41 us: body(): arrived = jnp.stack([arrived, lax.ppermute(arrived, RING, back)])]
    ppermute x2 -> x0, waiting for transfers between devices: 1.55 us -> none  [the longest x1 1.54 us: body(): places = jnp.stack([places, lax.ppermute(places, RING, back)])]
    unnamed x22 -> x15, local copies, waits for them, and re-layouts: 5.16 us -> 5.29 us
  transfers between devices with their start and end apart: 3 -> 0, of which waited for: 2 -> 0; matrix products, arithmetic and copies ran while one was open for 0% -> 0% of each run, Pallas kernels for 0% -> 0%
where the time goes in v1:
time: 75.8 us; the launch traced here: 75.6 us
  Pallas kernels  68.3 us (90%)
  local copies, waits for them, and re-layouts  6.56 us (9%)
    pallas_call x1, Pallas kernels, body(): pl.pallas_call(layer_kernel, out_shape=(jax.ShapeDtypeStruct((points, wid...  27.6 us
    pallas_call x1, Pallas kernels, body(): pl.pallas_call(sum_kernel, out_shape=jax.ShapeDtypeStruct((3 * d, width),...  25.4 us
    pallas_call x1, Pallas kernels, body(): pl.pallas_call(order_kernel, out_shape=jax.ShapeDtypeStruct((2, points, f...  15.3 us
    unnamed x15, local copies, waits for them, and re-layouts  5.29 us

profile of v1, /device:TPU:0, one launch (start us, length us, event | category | flops | bytes accessed | tf_op | source)
XLA Modules:
  0.0 75.6 jit_solution(5375245855930356634)
XLA Ops:
  0.6 0.0 copy-start
  0.6 0.8 %copy.13 = s32[4,8,4]{2,1,0:T(8,128)S(1)} copy(s32[4,8,4]{1,2,0:T(4,128)} %param.14) | data formatting | bytes 1024 | tf_op args[6]
  1.5 0.1 reshape.14.up_ref
  1.6 0.0 copy-start.1
  1.6 0.9 %copy-done.1 = bf16[1024,128]{1,0:T(8,128)(2,1)S(1)} copy-done((bf16[1024,128]{1,0:T(8,128)(2,1)S(1)}, bf16[1024,128]{1,0:T(8,128)(2,1)}, u32[]{:S(2)}) %copy-start.1) | copy-done | bytes 262168
  2.5 0.0 copy-start.6
  2.5 0.7 copy-done.6
  3.2 0.0 copy-start.2
  3.2 15.3 %order.1.flowed_ref = bf16[2,1024,128]{2,1,0:T(8,128)(2,1)S(1)} custom-call(bf16[1024,128]{1,0:T(8,128)(2,1)S(1)} %copy-done.1, s32[8,1,128]{2,1,0:T(1,128)S(1)} %bitcast.1), custom_call_target="tpu_custom_call" | custom-call | tf_op jit(solution)/shard_map/order/pallas_call | solution.py:321
  18.6 0.0 copy-done
  18.6 0.0 copy-done.2
  18.6 0.0 copy-start.3
  18.6 0.9 %copy-done.3 = bf16[512,256]{1,0:T(8,128)(2,1)S(1)} copy-done((bf16[512,256]{1,0:T(8,128)(2,1)S(1)}, bf16[512,256]{1,0:T(8,128)(2,1)}, u32[]{:S(2)}) %copy-start.3) | copy-done | bytes 262168
  19.6 0.0 copy-start.4
  19.6 0.9 %copy-done.4 = bf16[512,256]{1,0:T(8,128)(2,1)S(1)} copy-done((bf16[512,256]{1,0:T(8,128)(2,1)S(1)}, bf16[512,256]{1,0:T(8,128)(2,1)}, u32[]{:S(2)}) %copy-start.4) | copy-done | bytes 262168
  20.5 0.0 copy-start.5
  20.5 0.9 %copy-done.5 = bf16[128,512]{1,0:T(8,128)(2,1)S(1)} copy-done((bf16[128,512]{1,0:T(8,128)(2,1)S(1)}, bf16[128,512]{1,0:T(8,128)(2,1)}, u32[]{:S(2)}) %copy-start.5) | copy-done | bytes 131096
  21.4 27.6 %layer.1 = (bf16[1024,256]{1,0:T(8,128)(2,1)}, bf16[1536,256]{1,0:T(8,128)(2,1)S(1)}) custom-call(s32[128]{0:T(128)S(1)} %reshape.14.up_ref, bf16[2,1024,128]{2,1,0:T(8,128)(2,1)S(1)} %order.1.flowed_ref, bf16[128,512]{1,0:T(8,128)(2,1)S(1)} %copy-done.5, bf16[512,256]{1,0:T(8,128)(2,1)S(1)} %copy-done.2, bf16[512,256]{1,0:T(8,128)(2,1)S(1)} %copy-done.3, ...), custom_call_target="tpu_custom_call" | custom-call | tf_op jit(solution)/shard_map/layer/pallas_call | solution.py:339
  49.0 25.4 %sum.1 = bf16[1536,256]{1,0:T(8,128)(2,1)S(1)} custom-call(bf16[1536,256]{1,0:T(8,128)(2,1)S(1)} %get-tuple-element.7.g_ref), custom_call_target="tpu_custom_call" | custom-call | tf_op jit(solution)/shard_map/sum/pallas_call | solution.py:358
  74.4 1.2 %fusion = (f32[512,256]{1,0:T(8,128)}, f32[512,256]{1,0:T(8,128)}, f32[512,256]{1,0:T(8,128)}) fusion(bf16[1536,256]{1,0:T(8,128)(2,1)S(1)} %sum.1), kind=kLoop, calls=%fused_computation | loop fusion | bytes 3145728 | tf_op jit(solution)/shard_map/slice | solution.py:371
Async XLA Ops:
  0.6 18.0 %copy-start = (bf16[1024,256]{1,0:T(8,128)(2,1)S(1)}, bf16[1024,256]{1,0:T(8,128)(2,1)}, u32[]{:S(2)}) copy-start(bf16[1024,256]{1,0:T(8,128)(2,1)} %grad_ref.1) | copy-start | bytes 1572868
  1.6 1.0 %copy-start.1 = (bf16[1024,128]{1,0:T(8,128)(2,1)S(1)}, bf16[1024,128]{1,0:T(8,128)(2,1)}, u32[]{:S(2)}) copy-start(bf16[1024,128]{1,0:T(8,128)(2,1)} %rows_ref.1) | copy-start | bytes 786436
  2.5 0.7 copy-start.6
  3.2 15.4 %copy-start.2 = (bf16[512,256]{1,0:T(8,128)(2,1)S(1)}, bf16[512,256]{1,0:T(8,128)(2,1)}, u32[]{:S(2)}) copy-start(bf16[512,256]{1,0:T(8,128)(2,1)} %wq_ref.1) | copy-start | bytes 786436
  18.6 1.0 %copy-start.3 = (bf16[512,256]{1,0:T(8,128)(2,1)S(1)}, bf16[512,256]{1,0:T(8,128)(2,1)}, u32[]{:S(2)}) copy-start(bf16[512,256]{1,0:T(8,128)(2,1)} %wk_ref.1) | copy-start | bytes 786436
  19.6 0.9 %copy-start.4 = (bf16[512,256]{1,0:T(8,128)(2,1)S(1)}, bf16[512,256]{1,0:T(8,128)(2,1)}, u32[]{:S(2)}) copy-start(bf16[512,256]{1,0:T(8,128)(2,1)} %wv_ref.1) | copy-start | bytes 786436
  20.5 0.9 %copy-start.5 = (bf16[128,512]{1,0:T(8,128)(2,1)S(1)}, bf16[128,512]{1,0:T(8,128)(2,1)}, u32[]{:S(2)}) copy-start(bf16[128,512]{1,0:T(8,128)(2,1)} %enc_ref.1) | copy-start | bytes 393220

commit v2 on v1

--- a/solution.py
+++ b/solution.py
@@ -20,14 +20,35 @@
 PIECES = 6
 
 
-def order_kernel(
-    rows_ref, index_ref, out_ref,
-    got, got_index, total, mine, following, sent, landed, sent_index, landed_index, halo,
+def front_kernel(
+    rows_ref, index_ref, enc_in, wq_in, wk_in, wv_in, grad_in,
+    normed_t, kv, kv_t, pairs,
+    got, got_index, total, mine, following, enc_ref, wq_ref, wk_ref, wv_ref, grad_ref, wkv, wq,
+    sent, landed, sent_index, landed_index, halo, local,
 ):
     peers, pair, _ = got.shape
     points = rows_ref.shape[0]
+    blocks, heads = pairs.shape[:2]
+    blk, hd = points // blocks, pairs.shape[3] // 2
     cores = lax.axis_size("section")
     me = lax.axis_index(RING)
+    own = pl.ds(pl.multiple_of(me * pair, pair), pair)
+    loads = [
+        pltpu.make_async_copy(src, dst, local.at[i])
+        for i, (src, dst) in enumerate(
+            (
+                (rows_ref.at[own], got.at[me]),
+                (index_ref.at[me], got_index.at[me]),
+                (grad_in, grad_ref),
+                (wk_in, wk_ref),
+                (wv_in, wv_ref),
+                (wq_in, wq_ref),
+                (enc_in, enc_ref),
+            )
+        )
+    ]
+    for load in loads:
+        load.start()
 
     def device(i):
         return {"seq": i // cores, "section": lax.rem(i, cores)}
@@ -64,7 +85,16 @@
         index.start()
         rows.start()
 
-    total[...] = place(index_ref[me], rows_ref[pl.ds(pl.multiple_of(me * pair, pair), pair), :])
+    for load in loads:
+        load.wait()
+    total[...] = place(got_index[me], got[me])
+    for h in range(heads):
+        one, to = slice(h * hd, (h + 1) * hd), slice(2 * h * hd, 2 * (h + 1) * hd)
+        wkv[:, to] = jnp.concatenate([wk_ref[:, one], wv_ref[:, one]], axis=1)
+        wq[:, to] = jnp.concatenate([wq_ref[:, one], jnp.zeros_like(wq_ref[:, one])], axis=1)
+        grads = grad_ref[:, one]
+        shifted = jnp.concatenate([jnp.zeros_like(grads), grads], axis=1)
+        pairs[:, h, blk:, :] = shifted.reshape(blocks, blk, 2 * hd)
 
     @pl.loop(1, peers)
     def _(i):
@@ -80,16 +110,38 @@
         mine, following, halo.at[0], halo.at[1], device_id=device(before), device_id_type=MESH
     )
     copy.start()
-    out_ref[0] = mine[...]
+
+    def project(part, flowed_ref):
+        for start in range(0, points, CHUNK):
+            flowed = flowed_ref[start : start + CHUNK, :]
+            encoded = jax.nn.gelu(dot(flowed, enc_ref[...])).astype(jnp.bfloat16)
+            wide = encoded.astype(jnp.float32)
+            mean = jnp.mean(wide * wide, axis=1, keepdims=True)
+            normed = (wide * lax.rsqrt(mean + 1e-05)).astype(jnp.bfloat16)
+            at = part * points + start
+            normed_t[:, at : at + CHUNK] = normed.T
+            projected = dot(normed, wkv[...]).astype(jnp.bfloat16)
+            turned = projected.T
+            for i in range(CHUNK // blk):
+                kv[at // blk + i] = projected[i * blk : (i + 1) * blk]
+                kv_t[at // blk + i] = turned[:, i * blk : (i + 1) * blk]
+            if part == 0:
+                queries = dot(normed, wq[...]).astype(jnp.bfloat16) * jnp.bfloat16(hd**-0.5)
+                for i in range(CHUNK // blk):
+                    for h in range(heads):
+                        pairs[start // blk + i, h, :blk, :] = queries[
+                            i * blk : (i + 1) * blk, h * 2 * hd : (h + 1) * 2 * hd
+                        ]
+
+    project(0, mine)
+    copy.wait()
+    project(1, following)
 
     @pl.loop(1, peers)
     def _(i):
         rows, index = send(lax.rem(me + i, peers), me)
         index.wait_send()
         rows.wait_send()
-
-    copy.wait()
-    out_ref[1] = following[...]
 
 
 def sum_kernel(g_ref, out_ref, beside, part, up, cross, whole, *sems):
@@ -211,50 +263,15 @@
             to_outer(t).wait_send()
 
 
-def layer_kernel(
-    up_ref, flowed_ref, enc_ref, wq_ref, wk_ref, wv_ref, grad_ref,
-    att_ref, g_ref,
-    normed_t, kv, kv_t, pairs, dq_t, *dkv,
-):
-    heads, blocks, slots = len(dkv), pairs.shape[0], 4
-    points, width = grad_ref.shape
+def layer_kernel(up_ref, normed_t, kv, kv_t, pairs, att_ref, g_ref, dq_t, *dkv):
+    heads, blocks, slots = len(dkv), pairs.shape[0], up_ref.shape[1]
+    points, width = att_ref.shape
+    d = normed_t.shape[0]
     hd = width // heads
     blk = points // blocks
     shard = lax.axis_index(RING)
-    wkv = jnp.concatenate(
-        [w[:, h * hd : (h + 1) * hd] for h in range(heads) for w in (wk_ref, wv_ref)], axis=1
-    )
-    no_weight = jnp.zeros((wq_ref.shape[0], hd), wq_ref.dtype)
-    wq = jnp.concatenate(
-        [w for h in range(heads) for w in (wq_ref[:, h * hd : (h + 1) * hd], no_weight)], axis=1
-    )
-    no_grad = jnp.zeros((points, hd), grad_ref.dtype)
     for h in range(heads):
-        shifted = jnp.concatenate([no_grad, grad_ref[:, h * hd : (h + 1) * hd]], axis=1)
-        pairs[:, h, blk:, :] = shifted.reshape(blocks, blk, 2 * hd)
         dkv[h][...] = jnp.zeros_like(dkv[h])
-
-    for part in range(2):
-        for start in range(0, points, CHUNK):
-            flowed = flowed_ref[part, start : start + CHUNK, :]
-            encoded = jax.nn.gelu(dot(flowed, enc_ref[...])).astype(jnp.bfloat16)
-            wide = encoded.astype(jnp.float32)
-            mean = jnp.mean(wide * wide, axis=1, keepdims=True)
-            normed = (wide * lax.rsqrt(mean + 1e-05)).astype(jnp.bfloat16)
-            at = part * points + start
-            normed_t[:, at : at + CHUNK] = normed.T
-            projected = dot(normed, wkv).astype(jnp.bfloat16)
-            turned = projected.T
-            for i in range(CHUNK // blk):
-                kv[at // blk + i] = projected[i * blk : (i + 1) * blk]
-                kv_t[at // blk + i] = turned[:, i * blk : (i + 1) * blk]
-            if part == 0:
-                queries = dot(normed, wq).astype(jnp.bfloat16) * jnp.bfloat16(hd**-0.5)
-                for i in range(CHUNK // blk):
-                    for h in range(heads):
-                        pairs[start // blk + i, h, :blk, :] = queries[
-                            i * blk : (i + 1) * blk, h * 2 * hd : (h + 1) * 2 * hd
-                        ]
 
     @pl.loop(0, blocks)
     def _(b):
@@ -262,7 +279,7 @@
         for h in range(heads):
             index, bias = [], []
             for j in range(slots):
-                entry = up_ref[(h * blocks + b) * slots + j]
+                entry = up_ref[h, j, b]
                 index.append(jnp.where(entry >= 0, entry - shard * blocks, 0))
                 bias.append(jnp.where(entry >= 0, 0.0, -1e30).astype(jnp.float32))
             cols = slice(h * 2 * hd, (h + 1) * 2 * hd)
@@ -292,7 +309,6 @@
         dq_t[b] = jnp.concatenate(query_grads, axis=0).astype(jnp.bfloat16)
 
     turned = jnp.concatenate([dq_t[b] for b in range(blocks)], axis=1)
-    d = enc_ref.shape[1]
     g_ref[:d] = (
         lax.dot_general(normed_t[:, :points], turned, NT, preferred_element_type=jnp.float32)
         * (hd**-0.5)
@@ -318,42 +334,58 @@
     pair = points // peers
     dma = pltpu.SemaphoreType.DMA
     vmem = pl.BlockSpec(memory_space=pltpu.VMEM)
-    flowed = pl.pallas_call(
-        order_kernel,
-        out_shape=jax.ShapeDtypeStruct((2, points, fin), features.dtype),
-        in_specs=[vmem] * 2,
-        out_specs=vmem,
+    bf16 = jnp.bfloat16
+    hbm = pl.BlockSpec(memory_space=pltpu.HBM)
+    shapes = (
+        (d, 2 * points), (2 * blocks, blk, 2 * width), (2 * blocks, 2 * width, blk),
+        (blocks, heads, 2 * blk, 2 * hd),
+    )
+    middle = pl.pallas_call(
+        front_kernel,
+        out_shape=[jax.ShapeDtypeStruct(shape, bf16) for shape in shapes],
+        in_specs=[hbm] * 7,
+        out_specs=[vmem] * 4,
         scratch_shapes=[
-            pltpu.VMEM((peers, pair, fin), features.dtype),
+            pltpu.VMEM((peers, pair, fin), bf16),
             pltpu.VMEM((peers, 1, pair), jnp.int32),
             pltpu.VMEM((points, fin), jnp.float32),
-            pltpu.VMEM((points, fin), features.dtype),
-            pltpu.VMEM((points, fin), features.dtype),
-            dma((peers,)), dma((peers,)), dma((peers,)), dma((peers,)), dma((2,)),
+            pltpu.VMEM((points, fin), bf16),
+            pltpu.VMEM((points, fin), bf16),
+            pltpu.VMEM((fin, d), bf16),
+            pltpu.VMEM((d, width), bf16),
+            pltpu.VMEM((d, width), bf16),
+            pltpu.VMEM((d, width), bf16),
+            pltpu.VMEM((points, width), bf16),
+            pltpu.VMEM((d, 2 * width), bf16),
+            pltpu.VMEM((d, 2 * width), bf16),
+            dma((peers,)), dma((peers,)), dma((peers,)), dma((peers,)), dma((2,)), dma((7,)),
         ],
         compiler_params=pltpu.CompilerParams(
-            collective_id=0, has_side_effects=True, vmem_limit_bytes=30 << 20
+            collective_id=0, has_side_effects=True, vmem_limit_bytes=36 << 20
         ),
-        name="order",
-    )(features, flow_index.reshape(peers, 1, pair))
+        name="front",
+    )(
+        *(
+            pltpu.with_memory_space_constraint(array, pltpu.HBM)
+            for array in (
+                features, flow_index.reshape(peers, 1, pair), enc_weight, q_weight, k_weight,
+                v_weight, grad_out,
+            )
+        )
+    )
     attended, partial = pl.pallas_call(
         layer_kernel,
-        out_shape=(jax.ShapeDtypeStruct((points, width), jnp.bfloat16), jax.ShapeDtypeStruct((3 * d, width), jnp.bfloat16)),
-        in_specs=[pl.BlockSpec(memory_space=pltpu.SMEM)] + [vmem] * 6,
+        out_shape=(
+            jax.ShapeDtypeStruct((points, width), bf16),
+            jax.ShapeDtypeStruct((3 * d, width), bf16),
+        ),
+        in_specs=[pl.BlockSpec(memory_space=pltpu.SMEM)] + [vmem] * 4,
         out_specs=(vmem,) * 2,
-        scratch_shapes=[
-            pltpu.VMEM((d, 2 * points), jnp.bfloat16),
-            pltpu.VMEM((2 * blocks, blk, 2 * width), jnp.bfloat16),
-            pltpu.VMEM((2 * blocks, 2 * width, blk), jnp.bfloat16),
-            pltpu.VMEM((blocks, heads, 2 * blk, 2 * hd), jnp.bfloat16),
-            pltpu.VMEM((blocks, width, blk), jnp.bfloat16),
-        ]
+        scratch_shapes=[pltpu.VMEM((blocks, width, blk), bf16)]
         + [pltpu.VMEM((2 * blocks, blk, 2 * hd), jnp.float32)] * heads,
-        compiler_params=pltpu.CompilerParams(vmem_limit_bytes=50 << 20),
+        compiler_params=pltpu.CompilerParams(vmem_limit_bytes=36 << 20),
         name="layer",
-    )(
-        upstream.reshape(-1), flowed, enc_weight, q_weight, k_weight, v_weight, grad_out
-    )
+    )(upstream.transpose(0, 2, 1), *middle)
     half = 3 * d // 2
     summed = pl.pallas_call(
         sum_kernel,

time: 75.8 us -> 68.8 us (0.908)
  local copies, waits for them, and re-layouts: 6.56 us -> 1.87 us
  Pallas kernels: 68.3 us -> 66.1 us
    pallas_call x1, Pallas kernels: 27.6 us -> 22.9 us  [body(): pl.pallas_call(layer_kernel, out_shape=(jax.ShapeDtypeStruct((points, wid...]
    unnamed x15 -> x2, local copies, waits for them, and re-layouts: 5.29 us -> 0.69 us
    pallas_call x1, Pallas kernels: 15.3 us -> 17.8 us  [body(): pl.pallas_call(front_kernel, out_shape=[jax.ShapeDtypeStruct(shape, bf16)...]
where the time goes in v2:
time: 68.8 us; the launch traced here: 68.6 us
  Pallas kernels  66.1 us (96%)
  local copies, waits for them, and re-layouts  1.87 us (3%)
    pallas_call x1, Pallas kernels, body(): pl.pallas_call(sum_kernel, out_shape=jax.ShapeDtypeStruct((3 * d, width),...  25.4 us
    pallas_call x1, Pallas kernels, body(): pl.pallas_call(layer_kernel, out_shape=(jax.ShapeDtypeStruct((points, wid...  22.9 us
    pallas_call x1, Pallas kernels, body(): pl.pallas_call(front_kernel, out_shape=[jax.ShapeDtypeStruct(shape, bf16)...  17.8 us

profile of v2, /device:TPU:0, one launch (start us, length us, event | category | flops | bytes accessed | tf_op | source)
XLA Modules:
  0.0 68.6 jit_solution(7078756736324404330)
XLA Ops:
  0.6 17.8 %front.1 = (bf16[512,2048]{1,0:T(8,128)(2,1)S(1)}, bf16[16,128,512]{2,1,0:T(8,128)(2,1)S(1)}, bf16[16,512,128]{2,1,0:T(8,128)(2,1)S(1)}, bf16[8,4,256,128]{3,2,1,0:T(8,128)(2,1)S(1)}) custom-call(bf16[1024,128]{1,0:T(8,128)(2,1)} %rows_ref.1, s32[8,1,128]{2,1,0:T(1,128)} %bitcast.3, bf16[128,512]{1,0:T(8,128)(2,1)} %enc_in.1, bf16[512,256]{1,0:T(8,128)(2,1)} %wq_in.1, ...), custom_call_target="tpu_custom_call" | custom-call | tf_op jit(solution)/shard_map/front/pallas_call | solution.py:343
  18.4 0.0 copy-start
  18.4 0.7 %copy-done = s32[4,8,4]{1,2,0:T(4,128)S(1)} copy-done((s32[4,8,4]{1,2,0:T(4,128)S(1)}, s32[4,8,4]{1,2,0:T(4,128)}, u32[]{:S(2)}) %copy-start) | copy-done | bytes 536
  19.1 22.9 %layer.1 = (bf16[1024,256]{1,0:T(8,128)(2,1)}, bf16[1536,256]{1,0:T(8,128)(2,1)S(1)}) custom-call(s32[4,4,8]{2,1,0:T(4,128)S(1)} %bitcast.2, bf16[512,2048]{1,0:T(8,128)(2,1)S(1)} %get-tuple-element.10.normed_t, bf16[16,128,512]{2,1,0:T(8,128)(2,1)S(1)} %get-tuple-element.11.kv, bf16[16,512,128]{2,1,0:T(8,128)(2,1)S(1)} %get-tuple-element.12.kv_t, ...), custom_call_target="tpu_custom_call" | custom-call | tf_op jit(solution)/shard_map/layer/pallas_call | solution.py:376
  42.1 25.4 %sum.1 = bf16[1536,256]{1,0:T(8,128)(2,1)S(1)} custom-call(bf16[1536,256]{1,0:T(8,128)(2,1)S(1)} %get-tuple-element.15.g_ref), custom_call_target="tpu_custom_call" | custom-call | tf_op jit(solution)/shard_map/sum/pallas_call | solution.py:390
  67.4 1.2 %fusion = (f32[512,256]{1,0:T(8,128)}, f32[512,256]{1,0:T(8,128)}, f32[512,256]{1,0:T(8,128)}) fusion(bf16[1536,256]{1,0:T(8,128)(2,1)S(1)} %sum.1), kind=kLoop, calls=%fused_computation | loop fusion | bytes 3145728 | tf_op jit(solution)/shard_map/slice | solution.py:403
Async XLA Ops:
  18.4 0.7 %copy-start = (s32[4,8,4]{1,2,0:T(4,128)S(1)}, s32[4,8,4]{1,2,0:T(4,128)}, u32[]{:S(2)}) copy-start(s32[4,8,4]{1,2,0:T(4,128)} %param.14) | copy-start | bytes 1540

commit v3 on v2

--- a/solution.py
+++ b/solution.py
@@ -17,7 +17,7 @@
 
 
 MESH = pl.DeviceIdType.MESH
-PIECES = 6
+PIECES = 4
 
 
 def front_kernel(
@@ -273,7 +273,7 @@
     for h in range(heads):
         dkv[h][...] = jnp.zeros_like(dkv[h])
 
-    @pl.loop(0, blocks)
+    @pl.loop(0, blocks, unroll=4)
     def _(b):
         attended, query_grads = [], []
         for h in range(heads):
@@ -385,7 +385,7 @@
         + [pltpu.VMEM((2 * blocks, blk, 2 * hd), jnp.float32)] * heads,
         compiler_params=pltpu.CompilerParams(vmem_limit_bytes=36 << 20),
         name="layer",
-    )(upstream.transpose(0, 2, 1), *middle)
+    )(pltpu.with_memory_space_constraint(upstream.transpose(0, 2, 1), pltpu.HBM), *middle)
     half = 3 * d // 2
     summed = pl.pallas_call(
         sum_kernel,

time: 68.8 us -> 66.1 us (0.961)
  Pallas kernels: 66.1 us -> 64 us
  local copies, waits for them, and re-layouts: 1.87 us -> 1.18 us
    pallas_call x1, Pallas kernels: 25.4 us -> 24.2 us  [body(): pl.pallas_call(sum_kernel, out_shape=jax.ShapeDtypeStruct((3 * d, width),...]
    pallas_call x1, Pallas kernels: 22.9 us -> 22.1 us  [body(): pl.pallas_call(layer_kernel, out_shape=(jax.ShapeDtypeStruct((points, wid...]
    unnamed x2 -> x0, local copies, waits for them, and re-layouts: 0.69 us -> none
where the time goes in v3:
time: 66.1 us; the launch traced here: 65.9 us
  Pallas kernels  64 us (97%)
  local copies, waits for them, and re-layouts  1.18 us (2%)
    pallas_call x1, Pallas kernels, body(): pl.pallas_call(sum_kernel, out_shape=jax.ShapeDtypeStruct((3 * d, width),...  24.2 us
    pallas_call x1, Pallas kernels, body(): pl.pallas_call(layer_kernel, out_shape=(jax.ShapeDtypeStruct((points, wid...  22.1 us
    pallas_call x1, Pallas kernels, body(): pl.pallas_call(front_kernel, out_shape=[jax.ShapeDtypeStruct(shape, bf16)...  17.8 us

profile of v3, /device:TPU:0, one launch (start us, length us, event | category | flops | bytes accessed | tf_op | source)
XLA Modules:
  0.0 65.9 jit_solution(6804281781708196395)
XLA Ops:
  0.6 17.8 %front.1 = (bf16[512,2048]{1,0:T(8,128)(2,1)S(1)}, bf16[16,128,512]{2,1,0:T(8,128)(2,1)S(1)}, bf16[16,512,128]{2,1,0:T(8,128)(2,1)S(1)}, bf16[8,4,256,128]{3,2,1,0:T(8,128)(2,1)S(1)}) custom-call(bf16[1024,128]{1,0:T(8,128)(2,1)} %rows_ref.1, s32[8,1,128]{2,1,0:T(1,128)} %bitcast.3, bf16[128,512]{1,0:T(8,128)(2,1)} %enc_in.1, bf16[512,256]{1,0:T(8,128)(2,1)} %wq_in.1, ...), custom_call_target="tpu_custom_call" | custom-call | tf_op jit(solution)/shard_map/front/pallas_call | solution.py:343
  18.4 22.1 %layer.1 = (bf16[1024,256]{1,0:T(8,128)(2,1)}, bf16[1536,256]{1,0:T(8,128)(2,1)S(1)}) custom-call(s32[4,4,8]{2,1,0:T(4,128)} %bitcast.2, bf16[512,2048]{1,0:T(8,128)(2,1)S(1)} %get-tuple-element.10.normed_t, bf16[16,128,512]{2,1,0:T(8,128)(2,1)S(1)} %get-tuple-element.11.kv, bf16[16,512,128]{2,1,0:T(8,128)(2,1)S(1)} %get-tuple-element.12.kv_t, ...), custom_call_target="tpu_custom_call" | custom-call | tf_op jit(solution)/shard_map/layer/pallas_call | solution.py:376
  40.5 24.2 %sum.1 = bf16[1536,256]{1,0:T(8,128)(2,1)S(1)} custom-call(bf16[1536,256]{1,0:T(8,128)(2,1)S(1)} %get-tuple-element.15.g_ref), custom_call_target="tpu_custom_call" | custom-call | tf_op jit(solution)/shard_map/sum/pallas_call | solution.py:390
  64.7 1.2 %fusion = (f32[512,256]{1,0:T(8,128)}, f32[512,256]{1,0:T(8,128)}, f32[512,256]{1,0:T(8,128)}) fusion(bf16[1536,256]{1,0:T(8,128)(2,1)S(1)} %sum.1), kind=kLoop, calls=%fused_computation | loop fusion | bytes 3145728 | tf_op jit(solution)/shard_map/slice | solution.py:403
